TPU v7x, 32 devices: a whole 2x2x4 slice. The times are simulated.
32 devices in a mesh: dp: 8 (over z, core), seq: 4 (over y, x).
Axes of the slice: x: 2, y: 2, z: 4, core: 2. Of those that a mesh axis runs over, the one named last changes fastest.
Arguments:
- ssd_input: bfloat16 [8192, 4096], P(('dp', 'seq')), parts along dimension 0, may hold values from -6 to 6
- gate_input: bfloat16 [8192, 4096], P(('dp', 'seq')), parts along dimension 0, may hold values from -6 to 6
- write_map: bfloat16 [8192, 512], P(('dp', 'seq')), parts along dimension 0, may hold values from -6 to 6
- read_map: bfloat16 [8192, 512], P(('dp', 'seq')), parts along dimension 0, may hold values from -6 to 6
- step_size: float32 [8192, 32], P(('dp', 'seq')), parts along dimension 0, may hold values from 0.002 to 12.8, as said below
- decay_log: float32 [32], replicated, as said below
- skip_gain: float32 [32], replicated, may hold values from 0.5 to 1.5
- norm_gain: bfloat16 [4096], replicated, may hold values from 0.099609375 to 1.8984375
- query_rows: bfloat16 [8192, 2048], P(('dp', 'seq')), parts along dimension 0, may hold values from -30 to 30
- key_rows: bfloat16 [8192, 512], P(('dp', 'seq')), parts along dimension 0, may hold values from -4 to 4
- value_rows: bfloat16 [8192, 512], P(('dp', 'seq')), parts along dimension 0, may hold values from -6 to 6
Outputs:
- ssd_out: bfloat16 [8192, 4096], P(('dp', 'seq')), parts along dimension 0
- attn_out: bfloat16 [8192, 2048], P(('dp', 'seq')), parts along dimension 0
There are 8 independent parts, one for each index of `dp`. A program takes and returns all parts, laid end to end along the dimension named above; an argument that names none is the same for every part. Nothing has to cross between parts.
Inputs may be any that keep to these rules, and one draw needn't show every extreme that they name: `step_size`: positive everywhere. Rates exp(decay_log) lie between 30 / 1024 and about 3.4.
All inputs are finite; a program needn't handle non-finite values.
Results may differ from a plain program's by a relative error of at most 0.0059.
Values may be sent and summed in bfloat16 or wider, within the bound.
A program may use at most 192 MiB of HBM per device.

v0:
```python
import math

import jax
import jax.numpy as jnp
from jax import lax
from jax.sharding import PartitionSpec as P

SSD_HEADS = 32
HEAD_DIM = 128
STATE = 128
GROUPS = 4
SPAN = 128
Q_HEADS = 16
KV_HEADS = 4
ATT_DIM = 128


def entering(value, axis, join, neutral):
    count, mine = (lax.axis_size(axis), lax.axis_index(axis))
    pieces = jax.tree.map(lambda part: lax.all_gather(part, axis), value)
    total = jax.tree.map(
        lambda part, zero: jnp.full_like(part, 0) + jnp.asarray(zero, part.dtype), value, neutral
    )

    def turn(position, total):
        longer = join(total, jax.tree.map(lambda part: part[position], pieces))
        return jax.tree.map(lambda new, old: jnp.where(position < mine, new, old), longer, total)

    return lax.fori_loop(0, count - 1, turn, total)


def gated_norm(mixed_out, gate_input, norm_gain):
    row_count = mixed_out.shape[0]
    gated_y = mixed_out * jax.nn.silu(gate_input.astype(jnp.float32))
    grouped = gated_y.reshape(row_count, GROUPS, -1)
    inverse = lax.rsqrt(jnp.mean(grouped * grouped, axis=-1, keepdims=True) + 1e-05)
    normed = (grouped * inverse).reshape(row_count, -1)
    return (normed * norm_gain.astype(jnp.float32)).astype(jnp.bfloat16)


def chain_join(earlier, later_part):
    return (
        earlier[0] + later_part[0],
        jnp.exp(later_part[0])[..., None, None] * earlier[1] + later_part[1],
    )


def ssd_local(ssd_input, write_map, read_map, step_size, decay_log, skip_gain):
    row_count = ssd_input.shape[0]
    n_spans = row_count // SPAN
    per_group = SSD_HEADS // GROUPS
    decay_rate = (-jnp.exp(decay_log)).reshape(GROUPS, per_group)
    inputs_x = ssd_input.reshape(n_spans, SPAN, GROUPS, per_group, HEAD_DIM)
    write_vals = write_map.reshape(n_spans, SPAN, GROUPS, STATE)
    read_vals = read_map.reshape(n_spans, SPAN, GROUPS, STATE)
    steps_dt = step_size.reshape(n_spans, SPAN, GROUPS, per_group)
    cumulative = jnp.cumsum(steps_dt * decay_rate, axis=1)
    causal = jnp.tril(jnp.ones((SPAN, SPAN), dtype=bool))
    log_gap = cumulative[:, :, None] - cumulative[:, None]
    decay_mat = jnp.where(causal[None, :, :, None, None], jnp.exp(jnp.minimum(log_gap, 0.0)), 0.0)
    intersection = jnp.einsum(
        "ctgn,csgn->ctsg", read_vals, write_vals, preferred_element_type=jnp.float32
    )
    weights = (intersection[..., None] * decay_mat * steps_dt[:, None]).astype(jnp.bfloat16)
    local_y = jnp.einsum(
        "ctsgj,csgjp->ctgjp", weights, inputs_x, preferred_element_type=jnp.float32
    )
    to_end = jnp.exp(cumulative[:, -1:] - cumulative) * steps_dt
    scaled = (to_end[..., None] * inputs_x).astype(jnp.bfloat16)
    span_states = jnp.einsum(
        "csgn,csgjp->cgjnp", write_vals, scaled, preferred_element_type=jnp.float32
    )
    span_decay = cumulative[:, -1]

    def advance(carry_state, pieces):
        piece_state, piece_decay = pieces
        return (jnp.exp(piece_decay)[..., None, None] * carry_state + piece_state, carry_state)

    zero_state = jnp.zeros((GROUPS, per_group, STATE, HEAD_DIM), jnp.float32)
    local_final, local_starts = lax.scan(advance, zero_state, (span_states, span_decay))
    device_decay = jnp.sum(span_decay, axis=0)
    prefix = entering(
        (device_decay, local_final),
        "seq",
        chain_join,
        (jnp.zeros_like(device_decay), jnp.zeros_like(local_final)),
    )
    incoming = prefix[1]
    before = jnp.cumsum(span_decay, axis=0) - span_decay
    starts = (local_starts + jnp.exp(before)[..., None, None] * incoming[None]).astype(jnp.bfloat16)
    carried = (
        jnp.einsum("ctgn,cgjnp->ctgjp", read_vals, starts, preferred_element_type=jnp.float32)
        * jnp.exp(cumulative)[..., None]
    )
    skip_heads = skip_gain.reshape(GROUPS, per_group)
    mixed_out = local_y + carried + skip_heads[:, :, None] * inputs_x
    return mixed_out.reshape(row_count, SSD_HEADS * HEAD_DIM)


def score_block(query_part, part_pos, key_block, value_block, k_pos, current):
    running, weight_sum, context_sum = current
    score_scale = ATT_DIM ** (-0.5)
    scores = (
        jnp.einsum("rhgd,khd->hgrk", query_part, key_block, preferred_element_type=jnp.float32)
        * score_scale
    )
    visible = k_pos[None, :] <= part_pos[:, None]
    scores = jnp.where(visible, scores, -1e30)
    newmax = jnp.maximum(running, jnp.max(scores, axis=-1))
    factor = jnp.exp(running - newmax)
    exps = jnp.where(visible, jnp.exp(scores - newmax[..., None]), 0.0)
    weight_sum = weight_sum * factor + jnp.sum(exps, axis=-1)
    update = jnp.einsum(
        "hgrk,khd->rhgd", exps.astype(jnp.bfloat16), value_block, preferred_element_type=jnp.float32
    )
    context_sum = context_sum * jnp.transpose(factor, (2, 0, 1))[..., None] + update
    return (newmax, weight_sum, context_sum)


def attend(local_q, q_pos, key_rows, value_rows):
    row_count = local_q.shape[0]
    group_size = Q_HEADS // KV_HEADS
    queries = local_q.reshape(row_count, KV_HEADS, group_size, ATT_DIM)
    quarter = row_count // 4
    query_parts = [queries[index_q * quarter : (index_q + 1) * quarter] for index_q in range(4)]
    part_positions = [q_pos[index_q * quarter : (index_q + 1) * quarter] for index_q in range(4)]
    part_last = [jnp.max(element_indices) for element_indices in part_positions]

    def fresh_state():
        return (
            jnp.full((KV_HEADS, group_size, quarter), -1e30, jnp.float32),
            jnp.zeros((KV_HEADS, group_size, quarter), jnp.float32),
            jnp.zeros((quarter, KV_HEADS, group_size, ATT_DIM), jnp.float32),
        )

    initial = (fresh_state(), fresh_state(), fresh_state(), fresh_state())
    key_piece = lax.all_gather(key_rows, "seq", axis=0, tiled=True)
    value_piece = lax.all_gather(value_rows, "seq", axis=0, tiled=True)
    piece_rows = key_piece.shape[0]
    block_rows = math.gcd(piece_rows, 512)
    key_all = key_piece.reshape(piece_rows, KV_HEADS, ATT_DIM)
    value_all = value_piece.reshape(piece_rows, KV_HEADS, ATT_DIM)

    def one_block(index_b, states):
        offset = index_b * block_rows
        key_block = lax.dynamic_slice_in_dim(key_all, offset, block_rows, 0)
        value_block = lax.dynamic_slice_in_dim(value_all, offset, block_rows, 0)
        k_pos = offset + jnp.arange(block_rows, dtype=jnp.int32)
        updated = []
        for index_q in range(4):
            compute = partial_block(
                query_parts[index_q], part_positions[index_q], key_block, value_block, k_pos
            )
            updated.append(
                lax.cond(
                    offset > part_last[index_q], lambda current: current, compute, states[index_q]
                )
            )
        return tuple(updated)

    result = lax.fori_loop(0, piece_rows // block_rows, one_block, initial)
    contexts = [state[2] / jnp.transpose(state[1], (2, 0, 1))[..., None] for state in result]
    context = jnp.concatenate(contexts, axis=0)
    return context.reshape(row_count, Q_HEADS * ATT_DIM).astype(jnp.bfloat16)


def partial_block(query_part, part_pos, key_block, value_block, k_pos):

    def compute(current):
        return score_block(query_part, part_pos, key_block, value_block, k_pos, current)

    return compute


def local(
    ssd_input,
    gate_input,
    write_map,
    read_map,
    step_size,
    decay_log,
    skip_gain,
    norm_gain,
    query_rows,
    key_rows,
    value_rows,
):
    mixed_out = ssd_local(ssd_input, write_map, read_map, step_size, decay_log, skip_gain)
    ssd_out = gated_norm(mixed_out, gate_input, norm_gain)
    row_count = query_rows.shape[0]
    my_index = lax.axis_index("seq")
    local_idx = jnp.arange(row_count, dtype=jnp.int32)
    q_pos = my_index * row_count + local_idx
    context = attend(query_rows, q_pos, key_rows, value_rows)
    return (ssd_out, context)


def solution(mesh):
    in_specs = (
        P(("dp", "seq"), None),
        P(("dp", "seq"), None),
        P(("dp", "seq"), None),
        P(("dp", "seq"), None),
        P(("dp", "seq"), None),
        P(),
        P(),
        P(),
        P(("dp", "seq"), None),
        P(("dp", "seq"), None),
        P(("dp", "seq"), None),
    )
    out_specs = (P(("dp", "seq"), None), P(("dp", "seq"), None))
    return jax.shard_map(local, mesh=mesh, in_specs=in_specs, out_specs=out_specs, check_vma=False)
```

profile of v0, /device:TPU:6, one launch (start us, length us, event | category | flops | bytes accessed | tf_op | source)
XLA Modules:
  0.0 203.7 jit_solution(1327101116900852310)
XLA Ops:
  7.2 1.8 copy.129
  9.1 1.8 copy.130
  12.5 1.0 copy.116
  14.0 2.1 %fusion.93 = (f32[2,128,4,8]{3,2,1,0:T(4,128)}, f32[2,128,4,8]{3,2,1,0:T(4,128)S(1)}) fusion(f32[2,128,4,8]{3,2,1,0:T(4,128)S(1)} %fusion.94, f32[2,128,4,8]{3,2,1,0:T(4,128)} %copy.116, f32[2,4,8]{2,1,0:T(4,128)S(1)} %get-tuple-element.1283), kind=kLoop, calls=%fused_computation.149 | loop fusion | flops 16384 | bytes 131328 | tf_op jit(solution)/shard_map/exp | solution.py:93
  16.3 3.5 %copy.158 = bf16[32,8,32,128]{3,2,1,0:T(8,128)(2,1)} copy(bf16[32,8,32,128]{3,1,2,0:T(8,128)(2,1)} %bitcast.211) | data formatting | bytes 4194304
  19.9 5.4 %convolution_bitcast_fusion.4 = f32[2,4,8,128,128]{3,4,2,1,0:T(8,128)} fusion(f32[2,128,4,8]{1,3,2,0:T(8,128)S(1)} %copy.117, bf16[2,128,4,8,128]{4,3,2,1,0:T(8,128)(2,1)} %bitcast.197, bf16[2,128,4,128,1]{3,2,1,0,4:T(4,128)(2,1)S(1)} %bitcast.210), kind=kOutput, calls=%fused_computation.109 | convolution fusion | flops 271581184 | bytes 6586368 | tf_op jit(solution)/shard_map/csgn,csgjp->cgjnp/dot_general | solution.py:70
  25.3 18.8 %while.63 = (s32[]{:T(128)}, f32[4,8,128,128]{3,2,1,0:T(8,128)S(1)}, f32[2,4,8,128,128]{4,3,2,1,0:T(8,128)}, f32[2,4,8]{2,1,0:T(4,128)S(1)}, f32[2,4,8,128,128]{3,4,2,1,0:T(8,128)}, /*index=5*/s32[]{:T(128)}, s32[]{:T(128)}) while((s32[]{:T(128)}, f32[4,8,128,128]{3,2,1,0:T(8,128)S(1)}, f32[2,4,8,128,128]{4,3,2,1,0:T(8,128)}, ...), condition=%wide.region_2.3_spmd.clone, body=%wide.region_1.2_spmd.clone.sunk | while | flops 2097155 | bytes 35652600 | solution.py:80
  25.3 1.5 bitcast_dynamic-update-slice_fusion.2
  26.8 1.5 copy-done.1
  28.2 1.5 constant_dynamic-slice_fusion.6
  29.7 3.0 %copy.181 = f32[1,4,8,128,128]{4,3,2,1,0:T(8,128)} copy(f32[1,4,8,128,128]{3,4,2,1,0:T(8,128)} %constant_dynamic-slice_fusion.6) | data formatting | bytes 4194304 | tf_op jit(solution)/shard_map/while/body/jit(dynamic_index_in_dim)/dynamic_slice | solution.py:80
  32.7 2.0 bitcast_add_fusion.3
  34.8 1.5 bitcast_dynamic-update-slice_fusion.2
  36.2 1.5 copy-done.1
  37.7 1.5 constant_dynamic-slice_fusion.6
  39.2 2.9 %copy.181 = f32[1,4,8,128,128]{4,3,2,1,0:T(8,128)} copy(f32[1,4,8,128,128]{3,4,2,1,0:T(8,128)} %constant_dynamic-slice_fusion.6) | data formatting | bytes 4194304 | tf_op jit(solution)/shard_map/while/body/jit(dynamic_index_in_dim)/dynamic_slice | solution.py:80
  42.1 2.0 bitcast_add_fusion.3
  44.1 1.3 copy-done
  45.7 2.2 %fusion.92 = (bf16[64,2048]{1,0:T(8,128)(2,1)}, bf16[64,2048]{1,0:T(8,128)(2,1)}, bf16[64,2048]{1,0:T(8,128)(2,1)S(1)}, bf16[64,2048]{1,0:T(8,128)(2,1)}) fusion(bf16[256,2048]{1,0:T(8,128)(2,1)} %param.33), kind=kLoop, calls=%fused_computation.148 | loop fusion | bytes 2097152 | tf_op jit(solution)/shard_map/slice | solution.py:125
  48.1 1.1 slice.46
  50.0 1.1 slice.49
  51.9 1.1 slice.52
  53.8 1.2 copy.125
  55.0 1.0 reshape.119
  56.1 1.1 convolution_bitcast_fusion.5
  57.2 2.0 %copy.110 = f32[2,128,128,4]{2,1,3,0:T(8,128)} copy(f32[2,128,128,4]{1,2,3,0:T(8,128)} %convolution_bitcast_fusion.5) | data formatting | bytes 1048576 | tf_op jit(solution)/shard_map/ctgn,csgn->ctsg/transpose | solution.py:61
  59.9 7.1 %all-gather.2 = f32[4,4,8]{2,1,0:T(4,128)S(1)} all-gather(f32[1,4,8]{2,1,0:T(4,128)S(1)} %bitcast.232), channel_id=2, replica_groups=mesh['dp'=8,'seq'=4] {'seq'}, dimensions={0}, use_global_device_ids=true | all-gather | bytes 640 | tf_op jit(solution)/shard_map/all_gather | solution.py:20
  67.0 1.2 slice_reduce_fusion.1
  68.8 4.6 %fusion.72 = f32[2,4,8,128,128]{4,3,2,1,0:T(8,128)} fusion(f32[2,128,4,8]{1,3,2,0:T(8,128)S(1)} %copy.114, f32[2,128,4,8]{1,3,2,0:T(8,128)S(1)} %copy.112, f32[2,128,128,4]{2,1,3,0:T(8,128)} %copy.110, pred[128,128]{1,0:T(8,128)(4,1)S(1)} %iota_compare_fusion, bf16[2,128,4,8,128]{4,3,2,1,0:T(8,128)(2,1)} %bitcast.198), kind=kOutput, calls=%fused_computation.110 | convolution fusion | flops 274726912 | bytes 6897664 | tf_op jit(solution)/shard_map/ctsgj,csgjp->ctgjp/dot_general | solution.py:65
  77.0 46.6 %while.62 = (s32[]{:T(128)}, f32[4,4,64]{2,1,0:T(4,128)S(1)}, f32[4,4,64]{2,1,0:T(4,128)S(1)}, f32[64,4,4,128]{3,0,2,1:T(8,128)}, f32[4,4,64]{2,1,0:T(4,128)S(1)...) while((s32[]{:T(128)}, f32[4,4,64]{2,1,0:T(4,128)S(1)}, ...), condition=%wide.region_29.30_spmd, body=%wide.region_12.29_spmd.sunk | while | flops 1102197248 | bytes 64761988 | solution.py:161
  77.0 2.2 %constant_dynamic-slice_fusion.5 = (bf16[512,4,128]{0,2,1:T(8,128)(2,1)S(1)}, bf16[512,4,128]{0,2,1:T(8,128)(2,1)}) fusion(bf16[1024,4,128]{0,2,1:T(8,128)(2,1)} %get-tuple-element.1399, s32[]{:T(128)S(6)} %select_n.135, bf16[1024,4,128]{0,2,1:T(8,128)(2,1)} %get-tuple-element.1398), kind=kLoop, calls=%fused_computation.85.clone.1 | loop fusion | bytes 2097156 | tf_op jit(solution)/shard_map/while/body/eval_jaxpr/dynamic_slice | solution.py:147
  79.2 1.4 copy.179
  82.4 4.2 %conditional.10 = (f32[4,4,64]{2,1,0:T(4,128)S(1)}, f32[4,4,64]{2,1,0:T(4,128)S(1)}, f32[64,4,4,128]{3,0,2,1:T(8,128)}) conditional(s32[]{:T(128)} %convert_element_type.118, (s32[512]{0:T(512)S(1)}, s32[64]{0:T(128)S(1)}, bf16[512,4,128]{2,0,1:T(8,128)(2,1)S(1)}, bf16[64,4,4,128]{3,0,2,1:T(8,128)(2,1)}, f32[4,4,64]{2,1,0:T(4,128)S(1)}, ...), branch_computations={%region_21.23_spmd, %region_24.24_spmd} | conditional | flops 275549184 | bytes 15133036 | solution.py:155
  82.5 1.6 fusion.32
  87.1 4.1 %conditional.11 = (f32[4,4,64]{2,1,0:T(4,128)S(1)}, f32[4,4,64]{2,1,0:T(4,128)S(1)}, f32[64,4,4,128]{3,0,2,1:T(8,128)}) conditional(s32[]{:T(128)} %convert_element_type.119, (s32[512]{0:T(512)S(1)}, s32[64]{0:T(128)S(1)}, bf16[512,4,128]{2,0,1:T(8,128)(2,1)S(1)}, bf16[64,4,4,128]{3,0,2,1:T(8,128)(2,1)}, f32[4,4,64]{2,1,0:T(4,128)S(1)}, ...), branch_computations={%region_25.27_spmd, %region_28.28_spmd} | conditional | flops 275549184 | bytes 15133036 | solution.py:155
  87.3 1.6 fusion.48
  91.9 4.1 %conditional.9 = (f32[4,4,64]{2,1,0:T(4,128)S(1)}, f32[4,4,64]{2,1,0:T(4,128)S(1)}, f32[64,4,4,128]{3,0,2,1:T(8,128)}) conditional(s32[]{:T(128)} %convert_element_type.117, (s32[512]{0:T(512)S(1)}, s32[64]{0:T(128)S(1)}, bf16[512,4,128]{2,0,1:T(8,128)(2,1)S(1)}, bf16[64,4,4,128]{3,0,2,1:T(8,128)(2,1)}, f32[4,4,64]{2,1,0:T(4,128)S(1)}, ...), branch_computations={%region_17.19_spmd, %region_20.20_spmd} | conditional | flops 275549184 | bytes 15133036 | solution.py:155
  92.0 1.6 fusion.16
  96.7 3.7 %conditional.8 = (f32[4,4,64]{2,1,0:T(4,128)S(1)}, f32[4,4,64]{2,1,0:T(4,128)S(1)}, f32[64,4,4,128]{3,0,2,1:T(8,128)}) conditional(s32[]{:T(128)} %convert_element_type.116, (s32[512]{0:T(512)S(1)}, s32[64]{0:T(128)}, bf16[512,4,128]{2,0,1:T(8,128)(2,1)S(1)}, bf16[64,4,4,128]{3,0,2,1:T(8,128)(2,1)S(1)}, f32[4,4,64]{2,1,0:T(4,128)S(1)}, ...), branch_computations={%region_13.15_spmd, %region_16.16_spmd} | conditional | flops 275549184 | bytes 15133036 | solution.py:155
  100.4 2.1 %constant_dynamic-slice_fusion.5 = (bf16[512,4,128]{0,2,1:T(8,128)(2,1)S(1)}, bf16[512,4,128]{0,2,1:T(8,128)(2,1)}) fusion(bf16[1024,4,128]{0,2,1:T(8,128)(2,1)} %get-tuple-element.1399, s32[]{:T(128)S(6)} %select_n.135, bf16[1024,4,128]{0,2,1:T(8,128)(2,1)} %get-tuple-element.1398), kind=kLoop, calls=%fused_computation.85.clone.1 | loop fusion | bytes 2097156 | tf_op jit(solution)/shard_map/while/body/eval_jaxpr/dynamic_slice | solution.py:147
  102.5 1.3 copy.179
  105.5 4.2 %conditional.10 = (f32[4,4,64]{2,1,0:T(4,128)S(1)}, f32[4,4,64]{2,1,0:T(4,128)S(1)}, f32[64,4,4,128]{3,0,2,1:T(8,128)}) conditional(s32[]{:T(128)} %convert_element_type.118, (s32[512]{0:T(512)S(1)}, s32[64]{0:T(128)S(1)}, bf16[512,4,128]{2,0,1:T(8,128)(2,1)S(1)}, bf16[64,4,4,128]{3,0,2,1:T(8,128)(2,1)}, f32[4,4,64]{2,1,0:T(4,128)S(1)}, ...), branch_computations={%region_21.23_spmd, %region_24.24_spmd} | conditional | flops 275549184 | bytes 15133036 | solution.py:155
  105.6 1.6 fusion.32
  110.3 4.2 %conditional.11 = (f32[4,4,64]{2,1,0:T(4,128)S(1)}, f32[4,4,64]{2,1,0:T(4,128)S(1)}, f32[64,4,4,128]{3,0,2,1:T(8,128)}) conditional(s32[]{:T(128)} %convert_element_type.119, (s32[512]{0:T(512)S(1)}, s32[64]{0:T(128)S(1)}, bf16[512,4,128]{2,0,1:T(8,128)(2,1)S(1)}, bf16[64,4,4,128]{3,0,2,1:T(8,128)(2,1)}, f32[4,4,64]{2,1,0:T(4,128)S(1)}, ...), branch_computations={%region_25.27_spmd, %region_28.28_spmd} | conditional | flops 275549184 | bytes 15133036 | solution.py:155
  110.4 1.6 fusion.48
  115.1 4.1 %conditional.9 = (f32[4,4,64]{2,1,0:T(4,128)S(1)}, f32[4,4,64]{2,1,0:T(4,128)S(1)}, f32[64,4,4,128]{3,0,2,1:T(8,128)}) conditional(s32[]{:T(128)} %convert_element_type.117, (s32[512]{0:T(512)S(1)}, s32[64]{0:T(128)S(1)}, bf16[512,4,128]{2,0,1:T(8,128)(2,1)S(1)}, bf16[64,4,4,128]{3,0,2,1:T(8,128)(2,1)}, f32[4,4,64]{2,1,0:T(4,128)S(1)}, ...), branch_computations={%region_17.19_spmd, %region_20.20_spmd} | conditional | flops 275549184 | bytes 15133036 | solution.py:155
  115.2 1.6 fusion.16
  119.8 3.7 %conditional.8 = (f32[4,4,64]{2,1,0:T(4,128)S(1)}, f32[4,4,64]{2,1,0:T(4,128)S(1)}, f32[64,4,4,128]{3,0,2,1:T(8,128)}) conditional(s32[]{:T(128)} %convert_element_type.116, (s32[512]{0:T(512)S(1)}, s32[64]{0:T(128)}, bf16[512,4,128]{2,0,1:T(8,128)(2,1)S(1)}, bf16[64,4,4,128]{3,0,2,1:T(8,128)(2,1)S(1)}, f32[4,4,64]{2,1,0:T(4,128)S(1)}, ...), branch_computations={%region_13.15_spmd, %region_16.16_spmd} | conditional | flops 275549184 | bytes 15133036 | solution.py:155
  123.5 1.5 divide_convert_fusion
  125.1 1.5 divide_convert_fusion.2
  127.5 1.6 convert_element_type.73
  129.1 25.3 %all-gather.11.cloned.1.call-done = f32[16,8,128,128]{3,2,1,0:T(8,128)} async-done(((f32[4,8,128,128]{3,2,1,0:T(8,128)}), f32[16,8,128,128]{3,2,1,0:T(8,128)}) %all-gather.11.cloned.1.call-update) | async-done | bytes 8388624 | tf_op jit(solution)/shard_map/all_gather | solution.py:20
  154.5 6.4 %while.64 = (s32[]{:T(128)}, f32[4,8,128,128]{3,2,1,0:T(8,128)S(1)}, s32[]{:T(128)}, f32[4,4,8]{2,1,0:T(4,128)S(1)}, f32[4,4,8,128,128]{4,3,2,1,0:T(8,128)}, /*index=5*/s32[]{:T(128)}, s32[]{:T(128)}) while((s32[]{:T(128)}, f32[4,8,128,128]{3,2,1,0:T(8,128)S(1)}, s32[]{:T(128)}, f32[4,4,8]{2,1,0:T(4,128)S(1)}, ...), condition=%wide.region_6.7_spmd.clone, body=%wide.region_5.6_spmd.clone.sunk | while | flops 2097156 | bytes 6291945 | solution.py:29
  154.5 2.1 %fusion.101 = f32[4,8,128,128]{3,2,1,0:T(8,128)S(1)} fusion(f32[4,4,8,128,128]{4,3,2,1,0:T(8,128)} %get-tuple-element.1319, s32[]{:T(128)} %get-tuple-element.1308, f32[4,8,128,128]{3,2,1,0:T(8,128)S(1)} %get-tuple-element.1309, f32[4,8]{1,0:T(4,128)S(1)} %exponential_bitcast_fusion.5, pred[]{:T(512)S(6)} %compare.7, pred[]{:T(512)S(6)} %lt.43), kind=kLoop, calls=%fused_computation.92.clone.1 | loop fusion | flops 2097152 | bytes 6291590 | tf_op jit(solution)/shard_map/while/body/eval_jaxpr/jit(_where)/select_n | solution.py:27
  156.7 2.1 %fusion.101 = f32[4,8,128,128]{3,2,1,0:T(8,128)S(1)} fusion(f32[4,4,8,128,128]{4,3,2,1,0:T(8,128)} %get-tuple-element.1319, s32[]{:T(128)} %get-tuple-element.1308, f32[4,8,128,128]{3,2,1,0:T(8,128)S(1)} %get-tuple-element.1309, f32[4,8]{1,0:T(4,128)S(1)} %exponential_bitcast_fusion.5, pred[]{:T(512)S(6)} %compare.7, pred[]{:T(512)S(6)} %lt.43), kind=kLoop, calls=%fused_computation.92.clone.1 | loop fusion | flops 2097152 | bytes 6291590 | tf_op jit(solution)/shard_map/while/body/eval_jaxpr/jit(_where)/select_n | solution.py:27
  158.8 2.1 %fusion.101 = f32[4,8,128,128]{3,2,1,0:T(8,128)S(1)} fusion(f32[4,4,8,128,128]{4,3,2,1,0:T(8,128)} %get-tuple-element.1319, s32[]{:T(128)} %get-tuple-element.1308, f32[4,8,128,128]{3,2,1,0:T(8,128)S(1)} %get-tuple-element.1309, f32[4,8]{1,0:T(4,128)S(1)} %exponential_bitcast_fusion.5, pred[]{:T(512)S(6)} %compare.7, pred[]{:T(512)S(6)} %lt.43), kind=kLoop, calls=%fused_computation.92.clone.1 | loop fusion | flops 2097152 | bytes 6291590 | tf_op jit(solution)/shard_map/while/body/eval_jaxpr/jit(_where)/select_n | solution.py:27
  161.0 5.2 %fusion.66 = f32[2,128,4,8,128]{4,1,3,2,0:T(8,128)S(1)} fusion(f32[2,4,8,128,128]{4,3,2,1,0:T(8,128)} %fusion.72, f32[2,4,8,128,128]{4,3,2,1,0:T(8,128)} %get-tuple-element.711, f32[4,8]{1,0:T(4,128)S(1)} %copy-done.19, f32[2,128,4,8]{1,3,2,0:T(8,128)S(1)} %copy.125, f32[4,8,128,128]{3,2,1,0:T(8,128)S(1)} %get-tuple-element.713, ...), kind=kOutput, calls=%fused_computation.99 | convolution fusion | flops 276824064 | bytes 17072512 | tf_op jit(solution)/shard_map/ctgn,cgjnp->ctgjp/dot_general | solution.py:92
  166.2 4.4 %copy.126 = f32[2,128,4,8,128]{4,3,2,1,0:T(8,128)} copy(f32[2,128,4,8,128]{4,1,3,2,0:T(8,128)S(1)} %fusion.66) | data formatting | bytes 8388608 | tf_op jit(solution)/shard_map/add | solution.py:96
  170.6 5.1 %reshape.122 = f32[256,4096]{1,0:T(8,128)} reshape(f32[2,128,4,8,128]{4,3,2,1,0:T(8,128)} %copy.126) | data formatting | bytes 8388608 | tf_op jit(solution)/shard_map/reshape | solution.py:97
  175.7 5.3 %fusion.91 = f32[256,4096]{1,0:T(8,128)} fusion(f32[256,4096]{1,0:T(8,128)} %reshape.122, bf16[256,4096]{1,0:T(8,128)(2,1)S(1)} %copy-done.7), kind=kLoop, calls=%fused_computation.147 | loop fusion | flops 7340032 | bytes 10485760 | tf_op jit(solution)/shard_map/mul | solution.py:36
  181.0 6.0 %mul.233 = f32[256,4,1024]{2,1,0:T(4,128)} reshape(f32[256,4096]{1,0:T(8,128)} %fusion.91) | data formatting | bytes 8388608 | tf_op jit(solution)/shard_map/mul | solution.py:36
  187.0 2.8 %reduce_sum.55 = f32[256,4]{1,0:T(8,128)S(1)} reduce(f32[256,4,1024]{2,1,0:T(4,128)} %mul.233, f32[]{:T(128)} %constant.120.clone.1), dimensions={2}, to_apply=%region_7.8 | reduce | flops 1047552 | bytes 4198404 | tf_op jit(solution)/shard_map/reduce_sum | solution.py:36
  190.5 3.9 %copy.159 = f32[32,8,4,1024]{3,1,2,0:T(8,128)S(1)} copy(f32[32,8,4,1024]{3,2,1,0:T(4,128)S(1)} %bitcast.201) | data formatting | bytes 8388608
  194.3 2.8 %multiply_convert_fusion = bf16[256,4096]{1,0:T(8,128)(2,1)} fusion(f32[256,4096]{1,0:T(8,128)S(1)} %bitcast.200, f32[4096]{0:T(1024)S(1)} %convert_element_type.71, f32[256,4096]{1,0:T(8,128)S(1)} %copy-done.2, bf16[256,4096]{1,0:T(8,128)(2,1)S(1)} %copy-done.7), kind=kLoop, calls=%fused_computation.106 | loop fusion | flops 9437184 | bytes 12599296 | tf_op jit(solution)/shard_map/convert_element_type | solution.py:38
  (176 shorter events, 35.8 us)
Async XLA Ops:
  7.2 66.3 %all-gather.7.cloned.1.call-start = ((), (), s32[]{:S(2)}) async-start(), calls=%async_computation | async-start | bytes 1310720 | tf_op jit(solution)/shard_map/all_gather | solution.py:137
  9.1 64.4 %all-gather.9.cloned.1.call-start = ((), (), s32[]{:S(2)}) async-start(), calls=%async_computation.1 | async-start | bytes 1310720 | tf_op jit(solution)/shard_map/all_gather | solution.py:138
  10.9 143.6 %all-gather.11.cloned.1.call-start = ((), (), s32[]{:S(2)}) async-start(), calls=%async_computation.2 | async-start | bytes 10485760 | tf_op jit(solution)/shard_map/all_gather | solution.py:20
  16.3 3.5 %copy-start.18 = (bf16[256,512]{1,0:T(8,128)(2,1)S(1)}, bf16[256,512]{1,0:T(8,128)(2,1)}, u32[]{:S(2)}) copy-start(bf16[256,512]{1,0:T(8,128)(2,1)} %param.27) | copy-start | bytes 786436
  25.3 2.9 %copy-start.1 = (f32[2,4,8,128,128]{3,4,2,1,0:T(8,128)S(1)}, f32[2,4,8,128,128]{3,4,2,1,0:T(8,128)}, u32[]{:S(2)}) copy-start(f32[2,4,8,128,128]{3,4,2,1,0:T(8,128)} %get-tuple-element.1298) | copy-start | bytes 12582916 | tf_op jit(solution)/shard_map/while
  34.7 2.9 %copy-start.1 = (f32[2,4,8,128,128]{3,4,2,1,0:T(8,128)S(1)}, f32[2,4,8,128,128]{3,4,2,1,0:T(8,128)}, u32[]{:S(2)}) copy-start(f32[2,4,8,128,128]{3,4,2,1,0:T(8,128)} %get-tuple-element.1298) | copy-start | bytes 12582916 | tf_op jit(solution)/shard_map/while
  44.1 1.3 copy-start
  51.9 7.3 %copy-start.22 = (f32[32]{0:T(128)S(1)}, f32[32]{0:T(128)}, u32[]{:S(2)}) copy-start(f32[32]{0:T(128)} %param.31) | copy-start | bytes 388
  51.9 8.0 %copy-start.21 = (bf16[4096]{0:T(1024)(128)(2,1)S(1)}, bf16[4096]{0:T(1024)(128)(2,1)}, u32[]{:S(2)}) copy-start(bf16[4096]{0:T(1024)(128)(2,1)} %param.32) | copy-start | bytes 24580
  56.1 17.4 %copy-start.8 = (bf16[2,128,4,128]{3,2,1,0:T(4,128)(2,1)}, bf16[2,128,4,128]{3,2,1,0:T(4,128)(2,1)S(1)}, u32[]{:S(2)}) copy-start(bf16[2,128,4,128]{3,2,1,0:T(4,128)(2,1)S(1)} %reshape.119) | copy-start | bytes 786436
  82.5 2.3 %copy-start.3 = (bf16[512,4,128]{2,0,1:T(8,128)(2,1)S(1)}, bf16[512,4,128]{2,0,1:T(8,128)(2,1)}, u32[]{:S(2)}) copy-start(bf16[512,4,128]{2,0,1:T(8,128)(2,1)} %get-tuple-element.649) | copy-start | bytes 1572868 | tf_op jit(solution)/shard_map/while/body/eval_jaxpr/cond
  82.5 2.3 %copy-start.14 = (f32[64,4,4,128]{3,0,2,1:T(8,128)S(1)}, f32[64,4,4,128]{3,0,2,1:T(8,128)}, u32[]{:S(2)}) copy-start(f32[64,4,4,128]{3,0,2,1:T(8,128)} %get-tuple-element.648) | copy-start | bytes 1572868 | tf_op jit(solution)/shard_map/while/body/eval_jaxpr/cond
  85.7 0.8 copy-start.15
  87.2 2.3 %copy-start.4 = (bf16[512,4,128]{2,0,1:T(8,128)(2,1)S(1)}, bf16[512,4,128]{2,0,1:T(8,128)(2,1)}, u32[]{:S(2)}) copy-start(bf16[512,4,128]{2,0,1:T(8,128)(2,1)} %get-tuple-element.657) | copy-start | bytes 1572868 | tf_op jit(solution)/shard_map/while/body/eval_jaxpr/cond
  87.2 2.3 %copy-start.16 = (f32[64,4,4,128]{3,0,2,1:T(8,128)S(1)}, f32[64,4,4,128]{3,0,2,1:T(8,128)}, u32[]{:S(2)}) copy-start(f32[64,4,4,128]{3,0,2,1:T(8,128)} %get-tuple-element.656) | copy-start | bytes 1572868 | tf_op jit(solution)/shard_map/while/body/eval_jaxpr/cond
  90.5 0.8 copy-start.17
  92.0 2.3 %copy-start.5 = (bf16[512,4,128]{2,0,1:T(8,128)(2,1)S(1)}, bf16[512,4,128]{2,0,1:T(8,128)(2,1)}, u32[]{:S(2)}) copy-start(bf16[512,4,128]{2,0,1:T(8,128)(2,1)} %get-tuple-element.641) | copy-start | bytes 1572868 | tf_op jit(solution)/shard_map/while/body/eval_jaxpr/cond
  92.0 2.3 %copy-start.12 = (f32[64,4,4,128]{3,0,2,1:T(8,128)S(1)}, f32[64,4,4,128]{3,0,2,1:T(8,128)}, u32[]{:S(2)}) copy-start(f32[64,4,4,128]{3,0,2,1:T(8,128)} %get-tuple-element.640) | copy-start | bytes 1572868 | tf_op jit(solution)/shard_map/while/body/eval_jaxpr/cond
  95.2 0.8 copy-start.13
  97.4 1.3 copy-start.6
  97.4 1.3 copy-start.10
  99.6 0.8 copy-start.11
  105.6 2.3 %copy-start.3 = (bf16[512,4,128]{2,0,1:T(8,128)(2,1)S(1)}, bf16[512,4,128]{2,0,1:T(8,128)(2,1)}, u32[]{:S(2)}) copy-start(bf16[512,4,128]{2,0,1:T(8,128)(2,1)} %get-tuple-element.649) | copy-start | bytes 1572868 | tf_op jit(solution)/shard_map/while/body/eval_jaxpr/cond
  105.6 2.3 %copy-start.14 = (f32[64,4,4,128]{3,0,2,1:T(8,128)S(1)}, f32[64,4,4,128]{3,0,2,1:T(8,128)}, u32[]{:S(2)}) copy-start(f32[64,4,4,128]{3,0,2,1:T(8,128)} %get-tuple-element.648) | copy-start | bytes 1572868 | tf_op jit(solution)/shard_map/while/body/eval_jaxpr/cond
  108.8 0.8 copy-start.15
  110.4 2.3 %copy-start.4 = (bf16[512,4,128]{2,0,1:T(8,128)(2,1)S(1)}, bf16[512,4,128]{2,0,1:T(8,128)(2,1)}, u32[]{:S(2)}) copy-start(bf16[512,4,128]{2,0,1:T(8,128)(2,1)} %get-tuple-element.657) | copy-start | bytes 1572868 | tf_op jit(solution)/shard_map/while/body/eval_jaxpr/cond
  110.4 2.3 %copy-start.16 = (f32[64,4,4,128]{3,0,2,1:T(8,128)S(1)}, f32[64,4,4,128]{3,0,2,1:T(8,128)}, u32[]{:S(2)}) copy-start(f32[64,4,4,128]{3,0,2,1:T(8,128)} %get-tuple-element.656) | copy-start | bytes 1572868 | tf_op jit(solution)/shard_map/while/body/eval_jaxpr/cond
  113.6 0.8 copy-start.17
  115.2 2.3 %copy-start.5 = (bf16[512,4,128]{2,0,1:T(8,128)(2,1)S(1)}, bf16[512,4,128]{2,0,1:T(8,128)(2,1)}, u32[]{:S(2)}) copy-start(bf16[512,4,128]{2,0,1:T(8,128)(2,1)} %get-tuple-element.641) | copy-start | bytes 1572868 | tf_op jit(solution)/shard_map/while/body/eval_jaxpr/cond
  115.2 2.3 %copy-start.12 = (f32[64,4,4,128]{3,0,2,1:T(8,128)S(1)}, f32[64,4,4,128]{3,0,2,1:T(8,128)}, u32[]{:S(2)}) copy-start(f32[64,4,4,128]{3,0,2,1:T(8,128)} %get-tuple-element.640) | copy-start | bytes 1572868 | tf_op jit(solution)/shard_map/while/body/eval_jaxpr/cond
  118.4 0.8 copy-start.13
  120.5 1.3 copy-start.6
  120.5 1.3 copy-start.10
  122.7 0.8 copy-start.11
  154.5 6.4 %copy-start.9 = (bf16[2,128,4,128]{3,2,1,0:T(4,128)(2,1)S(1)}, bf16[2,128,4,128]{3,2,1,0:T(4,128)(2,1)}, u32[]{:S(2)}) copy-start(bf16[2,128,4,128]{3,2,1,0:T(4,128)(2,1)} %copy-done.8) | copy-start | bytes 786436
  154.5 6.4 %copy-start.19 = (f32[4,8]{1,0:T(4,128)S(1)}, f32[4,8]{1,0:T(4,128)}, u32[]{:S(2)}) copy-start(f32[4,8]{1,0:T(4,128)} %mul.227) | copy-start | bytes 388
  154.5 6.5 %copy-start.20 = (f32[2,4,8]{2,1,0:T(4,128)S(1)}, f32[2,4,8]{2,1,0:T(4,128)}, u32[]{:S(2)}) copy-start(f32[2,4,8]{2,1,0:T(4,128)} %fusion.85) | copy-start | bytes 772
  170.6 5.1 %copy-start.7 = (bf16[256,4096]{1,0:T(8,128)(2,1)S(1)}, bf16[256,4096]{1,0:T(8,128)(2,1)}, u32[]{:S(2)}) copy-start(bf16[256,4096]{1,0:T(8,128)(2,1)} %param.26) | copy-start | bytes 6291460
  190.5 3.9 %copy-start.2 = (f32[256,4096]{1,0:T(8,128)S(1)}, f32[256,4096]{1,0:T(8,128)}, u32[]{:S(2)}) copy-start(f32[256,4096]{1,0:T(8,128)} %reshape.122) | copy-start | bytes 12582916
Sparse Core Ops, SparseCore 0:
  9.8 26.7 all-gather.6
  38.4 26.4 all-gather.8
  66.8 87.6 all-gather.10
where the time goes:
time: 208 us; the launch traced here: 204 us
  local copies, waits for them, and re-layouts  77.4 us (37%)
  other arithmetic  39.9 us (19%)
  matrix products  33.8 us (16%)
  waiting for transfers between devices  25.4 us (12%)
  between operations  14 us (7%)
  blocking collectives  7.07 us (3%)
  loops' own time  5.94 us (3%)
    all_gather x1, waiting for transfers between devices, entering(): pieces = jax.tree.map(lambda part: lax.all_gather(part, axis), value)  25.3 us
    unnamed x24, local copies, waits for them, and re-layouts  12.3 us
    dot_general x8, matrix products, score_block(): jnp.einsum('rhgd,khd->hgrk', query_part, key_block, preferred_element_typ...  10.4 us
    dynamic_slice x4, local copies, waits for them, and re-layouts, ssd_local(): lax.scan(advance, zero_state, (span_states, span_decay))  8.87 us
    dot_general x8, matrix products, score_block(): jnp.einsum('hgrk,khd->rhgd', exps.astype(jnp.bfloat16), value_block, pref...  7.09 us
    all_gather x1, blocking collectives, entering(): pieces = jax.tree.map(lambda part: lax.all_gather(part, axis), value)  7.07 us
    cond x48, local copies, waits for them, and re-layouts  6.51 us
    dynamic_slice x4, local copies, waits for them, and re-layouts, one_block(): value_block = lax.dynamic_slice_in_dim(value_all, offset, block_rows, 0)  6.35 us
  transfers between devices with their start and end apart: 3, of which 1 were waited for; matrix products, arithmetic and copies ran while one was open for 47% of the time, Pallas kernels for 0%

commit v1 on v0

v1 whole, which is shorter than its diff:
```python
import functools
import math

import jax
import jax.numpy as jnp
from jax import lax
from jax.experimental import pallas as pl
from jax.experimental.pallas import tpu as pltpu
from jax.sharding import PartitionSpec as P

HEAD_DIM = 128
STATE = 128
GROUPS = 4
PER_GROUP = 8
SPAN = 128
Q_HEADS = 16
KV_HEADS = 4
REP = Q_HEADS // KV_HEADS
ATT_DIM = 128
WIDE = PER_GROUP * HEAD_DIM
F32 = jnp.float32
BF16 = jnp.bfloat16
LOWEST = 125.0 * math.log(2.0)
REACH = 250.0 * math.log(2.0)
NT = (((1,), (1,)), ((), ()))
TN = (((0,), (0,)), ((), ()))


def lanes(start, size):
    return pl.ds(pl.multiple_of(start, 128), size)


def coded(value, most):
    root = jnp.sqrt(jnp.abs(value) * (1.0 / most))
    size = jnp.exp(root * REACH - LOWEST)
    return jnp.where(value < 0.0, -size, size).astype(BF16)


def decoded(code, most):
    wide = code.astype(F32)
    root = jnp.maximum(jnp.log(jnp.abs(wide)) + LOWEST, 0.0) * (1.0 / REACH)
    size = root * root * most
    return jnp.where(wide < 0.0, -size, size)


def largest(value):
    column = jnp.max(jnp.abs(value), axis=0, keepdims=True)
    most = jnp.max(column, axis=1, keepdims=True)
    return jnp.broadcast_to(jnp.maximum(most, 1e-30), (1, 128))


def remote(src, dst, send, recv, target):
    return pltpu.make_async_remote_copy(
        src_ref=src,
        dst_ref=dst,
        send_sem=send,
        recv_sem=recv,
        device_id={"seq": target},
        device_id_type=pl.DeviceIdType.MESH,
    )


def kernel(
    n,
    n1,
    n2,
    x_ref,
    gate_ref,
    w_ref,
    r_ref,
    step_ref,
    dlog_ref,
    skip_ref,
    gain_ref,
    q_ref,
    k_ref,
    v_ref,
    ssd_ref,
    att_ref,
    kbuf,
    vbuf,
    row_s,
    col_s,
    row_d,
    col_d,
    row_m,
    col_m,
    fin,
    cum_g,
    te_g,
    ec_g,
    cum_t,
    dt_t,
    st0,
    inc,
    loc,
    acc,
    mx,
    ls,
    kv_send,
    kv_recv,
    row_send,
    row_recv,
    col_send,
    col_recv,
    rm_send,
    rm_recv,
    cm_send,
    cm_recv,
    rd_send,
    rd_recv,
    cd_send,
    cd_recv,
):
    me = lax.axis_index("seq")
    a = me // n2
    b = me % n2
    rows = x_ref.shape[0]
    spans = rows // SPAN
    scale = ATT_DIM**-0.5

    barrier = pltpu.get_barrier_semaphore()

    def greet(i, _):
        pl.semaphore_signal(
            barrier,
            inc=1,
            device_id={"seq": lax.rem(me + i, n)},
            device_id_type=pl.DeviceIdType.MESH,
        )
        return _

    lax.fori_loop(1, n, greet, 0)
    pl.semaphore_wait(barrier, n - 1)

    def k_copy(src, dst):
        return remote(k_ref, kbuf.at[src], kv_send.at[0, dst], kv_recv.at[0, src], dst)

    def v_copy(src, dst):
        return remote(v_ref, vbuf.at[src], kv_send.at[1, dst], kv_recv.at[1, src], dst)

    def send_kv(d, _):
        k_copy(me, d).start()
        v_copy(me, d).start()
        return _

    lax.fori_loop(me + 1, n, send_kv, 0)

    def row_needed(i):
        return (i != b) & ((i > b) | (a < n1 - 1))

    def row_comes(i):
        return (i != b) & ((i < b) | (a < n1 - 1))

    def row_copy(src, dst, g):
        return remote(
            row_s.at[src, g], row_s.at[src, g], row_send.at[dst, g], row_recv.at[src, g], a * n2 + dst
        )

    def rm_copy(src, dst, g):
        return remote(
            row_m.at[src, g], row_m.at[src, g], rm_send.at[dst, g], rm_recv.at[src, g], a * n2 + dst
        )

    def rd_copy(src, dst):
        return remote(row_d.at[src], row_d.at[src], rd_send.at[dst], rd_recv.at[src], a * n2 + dst)

    def col_copy(src, dst, g):
        return remote(
            col_s.at[src, g], col_s.at[src, g], col_send.at[dst, g], col_recv.at[src, g], dst * n2 + b
        )

    def cm_copy(src, dst, g):
        return remote(
            col_m.at[src, g], col_m.at[src, g], cm_send.at[dst, g], cm_recv.at[src, g], dst * n2 + b
        )

    def cd_copy(src, dst):
        return remote(col_d.at[src], col_d.at[src], cd_send.at[dst], cd_recv.at[src], dst * n2 + b)

    def each(lo, hi, needed, act):
        def body(i, _):
            @pl.when(needed(i))
            def _go():
                act(i)

            return _

        lax.fori_loop(lo, hi, body, 0)

    rate = -jnp.exp(dlog_ref[...])
    below = lax.broadcasted_iota(jnp.int32, (SPAN, SPAN), 0)
    along = lax.broadcasted_iota(jnp.int32, (SPAN, SPAN), 1)
    causal = below >= along
    tri = causal.astype(F32)
    total = jnp.zeros((GROUPS * PER_GROUP, 1), F32)
    for c in range(spans):
        at = slice(c * SPAN, (c + 1) * SPAN)
        dt = step_ref[at, :]
        cum = jnp.dot(tri, dt * rate, precision=lax.Precision.HIGHEST, preferred_element_type=F32)
        cum_tr = cum.T
        te = jnp.exp(cum[SPAN - 1 :, :] - cum) * dt
        ec = jnp.exp(cum)
        for g in range(GROUPS):
            hs = slice(g * PER_GROUP, (g + 1) * PER_GROUP)
            cum_g[g, at, :] = cum[:, hs]
            te_g[g, at, :] = te[:, hs]
            ec_g[g, at, :] = ec[:, hs]
        cum_t[:, at] = cum_tr
        dt_t[:, at] = dt.T
        total = total + cum_tr[:, SPAN - 1 :]
    for g in range(GROUPS):
        hs = slice(g * PER_GROUP, (g + 1) * PER_GROUP)
        row_d[b, g, :, :] = jnp.broadcast_to(jnp.exp(total[hs, :]), (PER_GROUP, 128))
    each(0, n2, row_needed, lambda i: rd_copy(b, i).start())

    def end_decay(c, g):
        ends = cum_t[pl.ds(pl.multiple_of(g * PER_GROUP, 8), PER_GROUP), c * SPAN : (c + 1) * SPAN]
        return jnp.exp(jnp.broadcast_to(ends[:, SPAN - 1 :], (PER_GROUP, 128)))

    def states(g, _):
        for c in range(spans):
            at = slice(c * SPAN, (c + 1) * SPAN)
            te = te_g[g, at, :]
            wv = w_ref[at, lanes(g * STATE, STATE)]
            ed = end_decay(c, g)
            scaled = []
            for j in range(PER_GROUP):
                xv = x_ref[at, lanes(g * WIDE + j * HEAD_DIM, HEAD_DIM)].astype(F32)
                scaled.append((te[:, j : j + 1] * xv).astype(BF16))
            for j in range(0, PER_GROUP, 2):
                fresh = lax.dot_general(
                    wv, jnp.concatenate(scaled[j : j + 2], axis=1), TN, preferred_element_type=F32
                )
                for o in range(2):
                    js = slice((j + o) * HEAD_DIM, (j + o + 1) * HEAD_DIM)
                    part = fresh[:, o * HEAD_DIM : (o + 1) * HEAD_DIM]
                    if c:
                        part = ed[j + o : j + o + 1, :] * st0[c - 1, g, :, js] + part
                    if c < spans - 1:
                        st0[c, g, :, js] = part
                    else:
                        fin[g, :, js] = part
                        most = largest(part)
                        row_m[b, g, j + o : j + o + 1, :] = most
                        row_s[b, g, :, js] = coded(part, most)

        def go(i):
            rm_copy(b, i, g).start()
            row_copy(b, i, g).start()

        each(0, n2, row_needed, go)
        return _

    lax.fori_loop(0, GROUPS, states, 0)

    def within(g, _):
        for c in range(spans):
            at = slice(c * SPAN, (c + 1) * SPAN)
            rv = r_ref[at, lanes(g * STATE, STATE)]
            wv = w_ref[at, lanes(g * STATE, STATE)]
            cross = lax.dot_general(rv, wv, NT, preferred_element_type=F32)
            hs = pl.ds(pl.multiple_of(g * PER_GROUP, 8), PER_GROUP)
            cum_rows = cum_t[hs, at]
            dt_rows = dt_t[hs, at]
            cum_cols = cum_g[g, at, :]
            for j in range(PER_GROUP):
                gap = cum_cols[:, j : j + 1] - cum_rows[j : j + 1, :]
                decay = jnp.exp(jnp.where(causal, jnp.minimum(gap, 0.0), -1e30))
                weights = (cross * decay * dt_rows[j : j + 1, :]).astype(BF16)
                xv = x_ref[at, lanes(g * WIDE + j * HEAD_DIM, HEAD_DIM)]
                y = jnp.dot(weights, xv, preferred_element_type=F32)
                loc[at, lanes(g * WIDE + j * HEAD_DIM, HEAD_DIM)] = (
                    y + skip_ref[g * PER_GROUP + j] * xv.astype(F32)
                )
        return _

    lax.fori_loop(0, GROUPS, within, 0)

    seen = lax.broadcasted_iota(jnp.int32, (rows, rows), 0) >= lax.broadcasted_iota(
        jnp.int32, (rows, rows), 1
    )

    def own(h, _):
        kv = k_ref[:, lanes(h * ATT_DIM, ATT_DIM)]
        vv = v_ref[:, lanes(h * ATT_DIM, ATT_DIM)]
        for r in range(REP):
            at = lanes((h * REP + r) * ATT_DIM, ATT_DIM)
            s = lax.dot_general(q_ref[:, at], kv, NT, preferred_element_type=F32) * scale
            s = jnp.where(seen, s, -1e30)
            top = jnp.max(s, axis=-1, keepdims=True)
            p = jnp.exp(s - top)
            mx[h * REP + r] = jnp.broadcast_to(top, (rows, 128))
            ls[h * REP + r] = jnp.broadcast_to(jnp.sum(p, axis=-1, keepdims=True), (rows, 128))
            acc[:, at] = jnp.dot(p.astype(BF16), vv, preferred_element_type=F32)
        return _

    lax.fori_loop(0, KV_HEADS, own, 0)

    each(0, n2, row_comes, lambda i: rd_copy(i, b).wait_recv())

    @pl.when(a < n1 - 1)
    def _row_total():
        col_d[a] = lax.fori_loop(
            0, n2, lambda i, d: d * row_d[i], jnp.ones((GROUPS, PER_GROUP, 128), F32)
        )

    each(0, n1, lambda i: i > a, lambda i: cd_copy(a, i).start())

    def row_phase(g, _):
        def come(i):
            rm_copy(i, b, g).wait_recv()
            row_copy(i, b, g).wait_recv()

        each(0, n2, row_comes, come)
        for j in range(PER_GROUP):
            js = slice(j * HEAD_DIM, (j + 1) * HEAD_DIM)

            def fold(i, t, j=j, js=js):
                new = decoded(row_s[i, g, :, js], row_m[i, g, j : j + 1, :])
                return row_d[i, g, j : j + 1, :] * t + new

            before = lax.fori_loop(0, b, fold, jnp.zeros((STATE, HEAD_DIM), F32))
            inc[g, :, js] = before

            @pl.when(a < n1 - 1)
            def _all(before=before, fold=fold, j=j, js=js):
                mine = row_d[b, g, j : j + 1, :] * before + fin[g, :, js]
                whole = lax.fori_loop(b + 1, n2, fold, mine)
                most = largest(whole)
                col_m[a, g, j : j + 1, :] = most
                col_s[a, g, :, js] = coded(whole, most)

        def go(i):
            cm_copy(a, i, g).start()
            col_copy(a, i, g).start()

        each(0, n1, lambda i: i > a, go)
        return _

    lax.fori_loop(0, GROUPS, row_phase, 0)

    def earlier(src, _):
        k_copy(src, me).wait_recv()
        v_copy(src, me).wait_recv()

        def heads(h, _):
            kv = kbuf[src, :, lanes(h * ATT_DIM, ATT_DIM)]
            vv = vbuf[src, :, lanes(h * ATT_DIM, ATT_DIM)]
            for r in range(REP):
                at = lanes((h * REP + r) * ATT_DIM, ATT_DIM)
                s = lax.dot_general(q_ref[:, at], kv, NT, preferred_element_type=F32) * scale
                old = mx[h * REP + r]
                top = jnp.maximum(old, jnp.max(s, axis=-1, keepdims=True))
                factor = jnp.exp(old - top)
                p = jnp.exp(s - jnp.concatenate([top] * (rows // 128), axis=1))
                mx[h * REP + r] = top
                ls[h * REP + r] = ls[h * REP + r] * factor + jnp.sum(p, axis=-1, keepdims=True)
                acc[:, at] = acc[:, at] * factor + jnp.dot(
                    p.astype(BF16), vv, preferred_element_type=F32
                )
            return _

        lax.fori_loop(0, KV_HEADS, heads, 0)
        return _

    lax.fori_loop(0, me, earlier, 0)

    def close(h, _):
        at = lanes(h * ATT_DIM, ATT_DIM)
        att_ref[:, at] = (acc[:, at] / ls[h]).astype(BF16)
        return _

    lax.fori_loop(0, Q_HEADS, close, 0)

    each(0, n1, lambda i: i < a, lambda i: cd_copy(i, a).wait_recv())

    def finish(g, _):
        def come(i):
            cm_copy(i, a, g).wait_recv()
            col_copy(i, a, g).wait_recv()

        each(0, n1, lambda i: i < a, come)
        pre = lax.fori_loop(0, b, lambda i, d: d * row_d[i, g], jnp.ones((PER_GROUP, 128), F32))
        for j in range(PER_GROUP):
            js = slice(j * HEAD_DIM, (j + 1) * HEAD_DIM)

            def fold(i, t, j=j, js=js):
                new = decoded(col_s[i, g, :, js], col_m[i, g, j : j + 1, :])
                return col_d[i, g, j : j + 1, :] * t + new

            above = lax.fori_loop(0, a, fold, jnp.zeros((STATE, HEAD_DIM), F32))
            inc[g, :, js] = inc[g, :, js] + pre[j : j + 1, :] * above
        before = jnp.ones((PER_GROUP, 128), F32)
        for c in range(spans):
            at = slice(c * SPAN, (c + 1) * SPAN)
            rv = r_ref[at, lanes(g * STATE, STATE)]
            ec = ec_g[g, at, :]
            square = jnp.zeros((SPAN, HEAD_DIM), F32)
            for j in range(0, PER_GROUP, 2):
                starts = []
                for o in range(2):
                    js = slice((j + o) * HEAD_DIM, (j + o + 1) * HEAD_DIM)
                    start = inc[g, :, js]
                    if c:
                        start = before[j + o : j + o + 1, :] * start + st0[c - 1, g, :, js]
                    starts.append(start.astype(BF16))
                read = jnp.dot(rv, jnp.concatenate(starts, axis=1), preferred_element_type=F32)
                for o in range(2):
                    hs = lanes(g * WIDE + (j + o) * HEAD_DIM, HEAD_DIM)
                    mixed = (
                        loc[at, hs]
                        + read[:, o * HEAD_DIM : (o + 1) * HEAD_DIM] * ec[:, j + o : j + o + 1]
                    )
                    v = gate_ref[at, hs].astype(F32)
                    gated = mixed * (v / (1.0 + jnp.exp(-v)))
                    loc[at, hs] = gated
                    square = square + gated * gated
            mean = jnp.sum(square, axis=-1, keepdims=True) / WIDE
            inverse = lax.rsqrt(mean + 1e-05)
            for j in range(PER_GROUP):
                hs = lanes(g * WIDE + j * HEAD_DIM, HEAD_DIM)
                ssd_ref[at, hs] = (loc[at, hs] * inverse * gain_ref[:, hs].astype(F32)).astype(BF16)
            before = before * end_decay(c, g)
        return _

    lax.fori_loop(0, GROUPS, finish, 0)

    def sent_kv(d, _):
        k_copy(me, d).wait_send()
        v_copy(me, d).wait_send()
        return _

    lax.fori_loop(me + 1, n, sent_kv, 0)
    each(0, n2, row_needed, lambda i: rd_copy(b, i).wait_send())
    each(0, n1, lambda i: i > a, lambda i: cd_copy(a, i).wait_send())

    def sent(g, _):
        def row_left(i):
            rm_copy(b, i, g).wait_send()
            row_copy(b, i, g).wait_send()

        def col_left(i):
            cm_copy(a, i, g).wait_send()
            col_copy(a, i, g).wait_send()

        each(0, n2, row_needed, row_left)
        each(0, n1, lambda i: i > a, col_left)
        return _

    lax.fori_loop(0, GROUPS, sent, 0)


def local(
    n,
    ssd_input,
    gate_input,
    write_map,
    read_map,
    step_size,
    decay_log,
    skip_gain,
    norm_gain,
    query_rows,
    key_rows,
    value_rows,
):
    n2 = math.isqrt(n)
    while n % n2:
        n2 -= 1
    n1 = n // n2
    rows = ssd_input.shape[0]
    spans = rows // SPAN
    heads = GROUPS * PER_GROUP
    vmem = pl.BlockSpec(memory_space=pltpu.VMEM)
    smem = pl.BlockSpec(memory_space=pltpu.SMEM)
    dma = pltpu.SemaphoreType.DMA
    return pl.pallas_call(
        functools.partial(kernel, n, n1, n2),
        out_shape=(
            jax.ShapeDtypeStruct(ssd_input.shape, BF16),
            jax.ShapeDtypeStruct(query_rows.shape, BF16),
        ),
        in_specs=[vmem, vmem, vmem, vmem, vmem, vmem, smem, vmem, vmem, vmem, vmem],
        out_specs=(vmem, vmem),
        scratch_shapes=[
            pltpu.VMEM((n,) + key_rows.shape, BF16),
            pltpu.VMEM((n,) + value_rows.shape, BF16),
            pltpu.VMEM((n2, GROUPS, STATE, WIDE), BF16),
            pltpu.VMEM((n1, GROUPS, STATE, WIDE), BF16),
            pltpu.VMEM((n2, GROUPS, PER_GROUP, 128), F32),
            pltpu.VMEM((n1, GROUPS, PER_GROUP, 128), F32),
            pltpu.VMEM((n2, GROUPS, PER_GROUP, 128), F32),
            pltpu.VMEM((n1, GROUPS, PER_GROUP, 128), F32),
            pltpu.VMEM((GROUPS, STATE, WIDE), F32),
            pltpu.VMEM((GROUPS, rows, PER_GROUP), F32),
            pltpu.VMEM((GROUPS, rows, PER_GROUP), F32),
            pltpu.VMEM((GROUPS, rows, PER_GROUP), F32),
            pltpu.VMEM((heads, rows), F32),
            pltpu.VMEM((heads, rows), F32),
            pltpu.VMEM((spans - 1, GROUPS, STATE, WIDE), F32),
            pltpu.VMEM((GROUPS, STATE, WIDE), F32),
            pltpu.VMEM(ssd_input.shape, F32),
            pltpu.VMEM(query_rows.shape, F32),
            pltpu.VMEM((Q_HEADS, rows, 128), F32),
            pltpu.VMEM((Q_HEADS, rows, 128), F32),
            dma((2, n)),
            dma((2, n)),
            dma((n2, GROUPS)),
            dma((n2, GROUPS)),
            dma((n1, GROUPS)),
            dma((n1, GROUPS)),
            dma((n2, GROUPS)),
            dma((n2, GROUPS)),
            dma((n1, GROUPS)),
            dma((n1, GROUPS)),
            dma((n2,)),
            dma((n2,)),
            dma((n1,)),
            dma((n1,)),
        ],
        compiler_params=pltpu.CompilerParams(
            collective_id=0, has_side_effects=True, vmem_limit_bytes=58 * 2**20
        ),
        cost_estimate=pl.CostEstimate(
            flops=4 * 10**9, bytes_accessed=12 * 2**20, transcendentals=6 * 10**6
        ),
        name="hybrid_cores",
    )(
        ssd_input,
        gate_input,
        write_map,
        read_map,
        step_size,
        decay_log.reshape(1, -1),
        skip_gain,
        norm_gain.reshape(1, -1),
        query_rows,
        key_rows,
        value_rows,
    )


def solution(mesh):
    split = P(("dp", "seq"), None)
    in_specs = (split, split, split, split, split, P(), P(), P(), split, split, split)
    body = functools.partial(local, mesh.shape["seq"])
    return jax.shard_map(
        body, mesh=mesh, in_specs=in_specs, out_specs=(split, split), check_vma=False
    )
```

time: 208 us -> 72.7 us (0.35)
  the two profiles are of different devices: /device:TPU:6 before, /device:TPU:18 now
where the time goes in v1:
time: 72.7 us; the launch traced here: 72.4 us
  Pallas kernels  64.8 us (89%)
  local copies, waits for them, and re-layouts  7.01 us (10%)
    pallas_call x1, Pallas kernels, local(): pl.pallas_call(functools.partial(kernel, n, n1, n2), out_shape=(jax.Shape...  64.8 us
    unnamed x5, local copies, waits for them, and re-layouts  5.7 us

profile of v1, /device:TPU:18, one launch (start us, length us, event | category | flops | bytes accessed | tf_op | source)
XLA Modules:
  0.0 72.4 jit_solution(8488640033241076518)
XLA Ops:
  0.6 1.3 %reshape.11.gain_ref = bf16[1,4096]{1,0:T(2,128)(2,1)} reshape(bf16[4096]{0:T(1024)(128)(2,1)} %param.18) | data formatting | bytes 16384 | tf_op jit(solution)/shard_map/reshape | solution.py:537
  1.9 1.5 %copy.13.step_ref = f32[256,32]{1,0:T(8,128)} copy(f32[256,32]{0,1:T(8,128)} %param.15) | data formatting | bytes 65536 | tf_op args[4]
  3.5 64.8 %hybrid_cores.1 = (bf16[256,4096]{1,0:T(8,128)(2,1)}, bf16[256,2048]{1,0:T(8,128)(2,1)}) custom-call(bf16[256,4096]{1,0:T(8,128)(2,1)} %x_ref.1, bf16[256,4096]{1,0:T(8,128)(2,1)} %gate_ref.1, bf16[256,512]{1,0:T(8,128)(2,1)} %w_ref.1, bf16[256,512]{1,0:T(8,128)(2,1)} %r_ref.1, f32[256,32]{1,0:T(8,128)} %copy.13.step_ref, f32[1,32]{1,0:T(1,128)} %bitcast.1, ...), custom_call_target="tpu_custom_call" | custom-call | flops 4000000000 | bytes 12582912 | tf_op jit(solution)/shard_map/hybrid_cores/pallas_call | solution.py:478
  68.2 0.0 copy-start
  68.2 3.2 %copy.16 = bf16[256,4096]{1,0:T(8,128)(2,1)} copy(bf16[256,4096]{1,0:T(8,128)(2,1)} %get-tuple-element.4) | data formatting | bytes 4194304
  71.5 0.0 copy-done
  71.5 1.0 %copy.17 = bf16[256,2048]{1,0:T(8,128)(2,1)} copy(bf16[256,2048]{1,0:T(8,128)(2,1)S(1)} %copy-done) | data formatting | bytes 2097152
Async XLA Ops:
  68.2 3.2 %copy-start = (bf16[256,2048]{1,0:T(8,128)(2,1)S(1)}, bf16[256,2048]{1,0:T(8,128)(2,1)}, u32[]{:S(2)}) copy-start(bf16[256,2048]{1,0:T(8,128)(2,1)} %get-tuple-element.5) | copy-start | bytes 3145732

commit v2 on v1

--- a/solution.py
+++ b/solution.py
@@ -64,15 +64,15 @@
     n,
     n1,
     n2,
-    x_ref,
-    gate_ref,
+    x_hbm,
+    gate_hbm,
     w_ref,
-    r_ref,
+    r_hbm,
     step_ref,
     dlog_ref,
     skip_ref,
     gain_ref,
-    q_ref,
+    q_hbm,
     k_ref,
     v_ref,
     ssd_ref,
@@ -86,6 +86,12 @@
     row_m,
     col_m,
     fin,
+    gains,
+    x_ref,
+    gate_ref,
+    r_ref,
+    q_ref,
+    load,
     cum_g,
     te_g,
     ec_g,
@@ -97,7 +103,10 @@
     acc,
     mx,
     ls,
-    kv_send,
+    key_row,
+    key_col,
+    val_row,
+    val_col,
     kv_recv,
     row_send,
     row_recv,
@@ -115,9 +124,17 @@
     me = lax.axis_index("seq")
     a = me // n2
     b = me % n2
-    rows = x_ref.shape[0]
+    rows = x_hbm.shape[0]
     spans = rows // SPAN
     scale = ATT_DIM**-0.5
+
+    loads = [
+        pltpu.make_async_copy(src, dst, load.at[i])
+        for i, (src, dst) in enumerate(
+            ((x_hbm, x_ref), (r_hbm, r_ref), (q_hbm, q_ref), (gate_hbm, gate_ref))
+        )
+    ]
+    loads[0].start()
 
     barrier = pltpu.get_barrier_semaphore()
 
@@ -133,51 +150,6 @@
     lax.fori_loop(1, n, greet, 0)
     pl.semaphore_wait(barrier, n - 1)
 
-    def k_copy(src, dst):
-        return remote(k_ref, kbuf.at[src], kv_send.at[0, dst], kv_recv.at[0, src], dst)
-
-    def v_copy(src, dst):
-        return remote(v_ref, vbuf.at[src], kv_send.at[1, dst], kv_recv.at[1, src], dst)
-
-    def send_kv(d, _):
-        k_copy(me, d).start()
-        v_copy(me, d).start()
-        return _
-
-    lax.fori_loop(me + 1, n, send_kv, 0)
-
-    def row_needed(i):
-        return (i != b) & ((i > b) | (a < n1 - 1))
-
-    def row_comes(i):
-        return (i != b) & ((i < b) | (a < n1 - 1))
-
-    def row_copy(src, dst, g):
-        return remote(
-            row_s.at[src, g], row_s.at[src, g], row_send.at[dst, g], row_recv.at[src, g], a * n2 + dst
-        )
-
-    def rm_copy(src, dst, g):
-        return remote(
-            row_m.at[src, g], row_m.at[src, g], rm_send.at[dst, g], rm_recv.at[src, g], a * n2 + dst
-        )
-
-    def rd_copy(src, dst):
-        return remote(row_d.at[src], row_d.at[src], rd_send.at[dst], rd_recv.at[src], a * n2 + dst)
-
-    def col_copy(src, dst, g):
-        return remote(
-            col_s.at[src, g], col_s.at[src, g], col_send.at[dst, g], col_recv.at[src, g], dst * n2 + b
-        )
-
-    def cm_copy(src, dst, g):
-        return remote(
-            col_m.at[src, g], col_m.at[src, g], cm_send.at[dst, g], cm_recv.at[src, g], dst * n2 + b
-        )
-
-    def cd_copy(src, dst):
-        return remote(col_d.at[src], col_d.at[src], cd_send.at[dst], cd_recv.at[src], dst * n2 + b)
-
     def each(lo, hi, needed, act):
         def body(i, _):
             @pl.when(needed(i))
@@ -187,6 +159,76 @@
             return _
 
         lax.fori_loop(lo, hi, body, 0)
+
+    def key_copy(src_a, dst_b):
+        src = src_a * n2 + b
+        return remote(
+            kbuf.at[src], kbuf.at[src], key_row.at[src_a, dst_b], kv_recv.at[0, src], a * n2 + dst_b
+        )
+
+    def key_down(dst_a):
+        return remote(k_ref, kbuf.at[me], key_col.at[dst_a], kv_recv.at[0, me], dst_a * n2 + b)
+
+    def key_own(dst_b):
+        return remote(k_ref, kbuf.at[me], key_row.at[a, dst_b], kv_recv.at[0, me], a * n2 + dst_b)
+
+    def value_copy(src_b, dst_a):
+        src = a * n2 + src_b
+        return remote(
+            vbuf.at[src], vbuf.at[src], val_col.at[src_b, dst_a], kv_recv.at[1, src], dst_a * n2 + b
+        )
+
+    def value_down(dst_a):
+        return remote(v_ref, vbuf.at[me], val_col.at[b, dst_a], kv_recv.at[1, me], dst_a * n2 + b)
+
+    def value_own(dst_b):
+        return remote(v_ref, vbuf.at[me], val_row.at[dst_b], kv_recv.at[1, me], a * n2 + dst_b)
+
+    def got(which, src):
+        return remote(k_ref, kbuf.at[src], key_col.at[0], kv_recv.at[which, src], src).wait_recv()
+
+    def below_me(i):
+        return i > a
+
+    def row_needed(i):
+        return (i != b) & ((i > b) | (a < n1 - 1))
+
+    def row_comes(i):
+        return (i != b) & ((i < b) | (a < n1 - 1))
+
+    each(0, n1, below_me, lambda i: key_down(i).start())
+    each(0, n2, row_needed, lambda i: value_own(i).start())
+    each(0, n1, below_me, lambda i: value_down(i).start())
+    for later in loads[1:]:
+        later.start()
+
+    def row_copy(src, dst, g):
+        return remote(
+            row_s.at[src, g], row_s.at[src, g], row_send.at[dst, g], row_recv.at[src, g], a * n2 + dst
+        )
+
+    def rm_copy(src, dst, g):
+        return remote(
+            row_m.at[src, g], row_m.at[src, g], rm_send.at[dst, g], rm_recv.at[src, g], a * n2 + dst
+        )
+
+    def rd_copy(src, dst):
+        return remote(row_d.at[src], row_d.at[src], rd_send.at[dst], rd_recv.at[src], a * n2 + dst)
+
+    def col_copy(src, dst, g):
+        return remote(
+            col_s.at[src, g], col_s.at[src, g], col_send.at[dst, g], col_recv.at[src, g], dst * n2 + b
+        )
+
+    def cm_copy(src, dst, g):
+        return remote(
+            col_m.at[src, g], col_m.at[src, g], cm_send.at[dst, g], cm_recv.at[src, g], dst * n2 + b
+        )
+
+    def cd_copy(src, dst):
+        return remote(col_d.at[src], col_d.at[src], cd_send.at[dst], cd_recv.at[src], dst * n2 + b)
+
+    gains[...] = gain_ref[...].astype(F32)
 
     rate = -jnp.exp(dlog_ref[...])
     below = lax.broadcasted_iota(jnp.int32, (SPAN, SPAN), 0)
@@ -196,7 +238,8 @@
     total = jnp.zeros((GROUPS * PER_GROUP, 1), F32)
     for c in range(spans):
         at = slice(c * SPAN, (c + 1) * SPAN)
-        dt = step_ref[at, :]
+        dt_rows = step_ref[:, at]
+        dt = dt_rows.T
         cum = jnp.dot(tri, dt * rate, precision=lax.Precision.HIGHEST, preferred_element_type=F32)
         cum_tr = cum.T
         te = jnp.exp(cum[SPAN - 1 :, :] - cum) * dt
@@ -207,7 +250,7 @@
             te_g[g, at, :] = te[:, hs]
             ec_g[g, at, :] = ec[:, hs]
         cum_t[:, at] = cum_tr
-        dt_t[:, at] = dt.T
+        dt_t[:, at] = dt_rows
         total = total + cum_tr[:, SPAN - 1 :]
     for g in range(GROUPS):
         hs = slice(g * PER_GROUP, (g + 1) * PER_GROUP)
@@ -252,7 +295,9 @@
         each(0, n2, row_needed, go)
         return _
 
+    loads[0].wait()
     lax.fori_loop(0, GROUPS, states, 0)
+    each(0, n2, lambda i: i > b, lambda i: key_own(i).start())
 
     def within(g, _):
         for c in range(spans):
@@ -275,8 +320,6 @@
                 )
         return _
 
-    lax.fori_loop(0, GROUPS, within, 0)
-
     seen = lax.broadcasted_iota(jnp.int32, (rows, rows), 0) >= lax.broadcasted_iota(
         jnp.int32, (rows, rows), 1
     )
@@ -295,8 +338,6 @@
             acc[:, at] = jnp.dot(p.astype(BF16), vv, preferred_element_type=F32)
         return _
 
-    lax.fori_loop(0, KV_HEADS, own, 0)
-
     each(0, n2, row_comes, lambda i: rd_copy(i, b).wait_recv())
 
     @pl.when(a < n1 - 1)
@@ -338,11 +379,44 @@
         each(0, n1, lambda i: i > a, go)
         return _
 
-    lax.fori_loop(0, GROUPS, row_phase, 0)
-
-    def earlier(src, _):
-        k_copy(src, me).wait_recv()
-        v_copy(src, me).wait_recv()
+    for later in loads[1:3]:
+        later.wait()
+
+    def hand_keys(src_a, _):
+        got(0, src_a * n2 + b)
+        each(0, n2, lambda i: i != b, lambda i: key_copy(src_a, i).start())
+        return _
+
+    lax.fori_loop(0, a, hand_keys, 0)
+
+    def hand_values(src_b):
+        got(1, a * n2 + src_b)
+        each(0, n1, below_me, lambda i: value_copy(src_b, i).start())
+
+    each(0, n2, row_comes, hand_values)
+
+    def turn(g, _):
+        within(g, 0)
+        own(g, 0)
+
+        @pl.when(a < n1 - 1)
+        def _first():
+            row_phase(g, 0)
+
+        return _
+
+    lax.fori_loop(0, GROUPS, turn, 0)
+
+    def earlier(back, _):
+        src = me - 1 - back
+
+        @pl.when(src % n2 != b)
+        def _key():
+            got(0, src)
+
+        @pl.when(src // n2 != a)
+        def _value():
+            got(1, src)
 
         def heads(h, _):
             kv = kbuf[src, :, lanes(h * ATT_DIM, ATT_DIM)]
@@ -373,6 +447,11 @@
 
     lax.fori_loop(0, Q_HEADS, close, 0)
 
+    @pl.when(a == n1 - 1)
+    def _last():
+        lax.fori_loop(0, GROUPS, row_phase, 0)
+
+    loads[3].wait()
     each(0, n1, lambda i: i < a, lambda i: cd_copy(i, a).wait_recv())
 
     def finish(g, _):
@@ -418,20 +497,31 @@
                     square = square + gated * gated
             mean = jnp.sum(square, axis=-1, keepdims=True) / WIDE
             inverse = lax.rsqrt(mean + 1e-05)
+            gain = gains[pl.ds(pl.multiple_of(g * PER_GROUP, 8), PER_GROUP), :]
             for j in range(PER_GROUP):
                 hs = lanes(g * WIDE + j * HEAD_DIM, HEAD_DIM)
-                ssd_ref[at, hs] = (loc[at, hs] * inverse * gain_ref[:, hs].astype(F32)).astype(BF16)
+                ssd_ref[at, hs] = (loc[at, hs] * inverse * gain[j : j + 1, :]).astype(BF16)
             before = before * end_decay(c, g)
         return _
 
     lax.fori_loop(0, GROUPS, finish, 0)
 
-    def sent_kv(d, _):
-        k_copy(me, d).wait_send()
-        v_copy(me, d).wait_send()
-        return _
-
-    lax.fori_loop(me + 1, n, sent_kv, 0)
+    each(0, n1, below_me, lambda i: key_down(i).wait_send())
+    each(0, n2, row_needed, lambda i: value_own(i).wait_send())
+    each(0, n1, below_me, lambda i: value_down(i).wait_send())
+    each(0, n2, lambda i: i > b, lambda i: key_own(i).wait_send())
+
+    def handed(src_a, _):
+        each(0, n2, lambda i: i != b, lambda i: key_copy(src_a, i).wait_send())
+        return _
+
+    lax.fori_loop(0, a, handed, 0)
+    each(
+        0,
+        n2,
+        row_comes,
+        lambda j: each(0, n1, below_me, lambda i: value_copy(j, i).wait_send()),
+    )
     each(0, n2, row_needed, lambda i: rd_copy(b, i).wait_send())
     each(0, n1, lambda i: i > a, lambda i: cd_copy(a, i).wait_send())
 
@@ -473,15 +563,16 @@
     spans = rows // SPAN
     heads = GROUPS * PER_GROUP
     vmem = pl.BlockSpec(memory_space=pltpu.VMEM)
+    hbm = pl.BlockSpec(memory_space=pl.ANY)
     smem = pl.BlockSpec(memory_space=pltpu.SMEM)
     dma = pltpu.SemaphoreType.DMA
     return pl.pallas_call(
         functools.partial(kernel, n, n1, n2),
         out_shape=(
-            jax.ShapeDtypeStruct(ssd_input.shape, BF16),
-            jax.ShapeDtypeStruct(query_rows.shape, BF16),
+            pltpu.VMEM(ssd_input.shape, BF16),
+            pltpu.VMEM(query_rows.shape, BF16),
         ),
-        in_specs=[vmem, vmem, vmem, vmem, vmem, vmem, smem, vmem, vmem, vmem, vmem],
+        in_specs=[hbm, hbm, vmem, hbm, vmem, vmem, smem, vmem, hbm, vmem, vmem],
         out_specs=(vmem, vmem),
         scratch_shapes=[
             pltpu.VMEM((n,) + key_rows.shape, BF16),
@@ -493,6 +584,12 @@
             pltpu.VMEM((n2, GROUPS, PER_GROUP, 128), F32),
             pltpu.VMEM((n1, GROUPS, PER_GROUP, 128), F32),
             pltpu.VMEM((GROUPS, STATE, WIDE), F32),
+            pltpu.VMEM((heads, HEAD_DIM), F32),
+            pltpu.VMEM(ssd_input.shape, BF16),
+            pltpu.VMEM(gate_input.shape, BF16),
+            pltpu.VMEM(read_map.shape, BF16),
+            pltpu.VMEM(query_rows.shape, BF16),
+            dma((4,)),
             pltpu.VMEM((GROUPS, rows, PER_GROUP), F32),
             pltpu.VMEM((GROUPS, rows, PER_GROUP), F32),
             pltpu.VMEM((GROUPS, rows, PER_GROUP), F32),
@@ -504,7 +601,10 @@
             pltpu.VMEM(query_rows.shape, F32),
             pltpu.VMEM((Q_HEADS, rows, 128), F32),
             pltpu.VMEM((Q_HEADS, rows, 128), F32),
-            dma((2, n)),
+            dma((n1, n2)),
+            dma((n1,)),
+            dma((n2,)),
+            dma((n2, n1)),
             dma((2, n)),
             dma((n2, GROUPS)),
             dma((n2, GROUPS)),
@@ -531,10 +631,10 @@
         gate_input,
         write_map,
         read_map,
-        step_size,
+        step_size.T,
         decay_log.reshape(1, -1),
         skip_gain,
-        norm_gain.reshape(1, -1),
+        norm_gain.reshape(-1, HEAD_DIM),
         query_rows,
         key_rows,
         value_rows,

time: 72.7 us -> 62 us (0.85)
  the two profiles are of different devices: /device:TPU:18 before, /device:TPU:6 now
where the time goes in v2:
time: 62 us; the launch traced here: 61.9 us
  Pallas kernels  58.9 us (95%)
  local copies, waits for them, and re-layouts  2.29 us (4%)
  between operations  0.64 us (1%)
    pallas_call x1, Pallas kernels, local(): pl.pallas_call(functools.partial(kernel, n, n1, n2), out_shape=(pltpu.VME...  58.9 us
    unnamed x2, local copies, waits for them, and re-layouts  2.29 us

profile of v2, /device:TPU:6, one launch (start us, length us, event | category | flops | bytes accessed | tf_op | source)
XLA Modules:
  0.0 61.9 jit_solution(7141338137989152330)
XLA Ops:
  0.6 58.9 %hybrid_cores.1 = (bf16[256,4096]{1,0:T(8,128)(2,1)S(1)}, bf16[256,2048]{1,0:T(8,128)(2,1)S(1)}) custom-call(bf16[256,4096]{1,0:T(8,128)(2,1)} %x_hbm.1, bf16[256,4096]{1,0:T(8,128)(2,1)} %gate_hbm.1, bf16[256,512]{1,0:T(8,128)(2,1)} %w_ref.1, bf16[256,512]{1,0:T(8,128)(2,1)} %r_hbm.1, f32[32,256]{1,0:T(8,128)} %bitcast.3, f32[1,32]{1,0:T(1,128)} %bitcast.5, ...), custom_call_target="tpu_custom_call" | custom-call | flops 4000000000 | bytes 12582912 | tf_op jit(solution)/shard_map/hybrid_cores/pallas_call | solution.py:569
  59.6 1.3 %copy.15 = bf16[256,4096]{1,0:T(8,128)(2,1)} copy(bf16[256,4096]{1,0:T(8,128)(2,1)S(1)} %get-tuple-element.2) | data formatting | bytes 4194304
  60.9 1.0 %copy.16 = bf16[256,2048]{1,0:T(8,128)(2,1)} copy(bf16[256,2048]{1,0:T(8,128)(2,1)S(1)} %get-tuple-element.3) | data formatting | bytes 2097152

commit v3 on v2

--- a/solution.py
+++ b/solution.py
@@ -261,6 +261,11 @@
         ends = cum_t[pl.ds(pl.multiple_of(g * PER_GROUP, 8), PER_GROUP), c * SPAN : (c + 1) * SPAN]
         return jnp.exp(jnp.broadcast_to(ends[:, SPAN - 1 :], (PER_GROUP, 128)))
 
+    def hand_keys(src_a, _):
+        got(0, src_a * n2 + b)
+        each(0, n2, lambda i: i != b, lambda i: key_copy(src_a, i).start())
+        return _
+
     def states(g, _):
         for c in range(spans):
             at = slice(c * SPAN, (c + 1) * SPAN)
@@ -292,6 +297,10 @@
             rm_copy(b, i, g).start()
             row_copy(b, i, g).start()
 
+        @pl.when(g == 1)
+        def _keys():
+            lax.fori_loop(0, a, hand_keys, 0)
+
         each(0, n2, row_needed, go)
         return _
 
@@ -381,13 +390,6 @@
 
     for later in loads[1:3]:
         later.wait()
-
-    def hand_keys(src_a, _):
-        got(0, src_a * n2 + b)
-        each(0, n2, lambda i: i != b, lambda i: key_copy(src_a, i).start())
-        return _
-
-    lax.fori_loop(0, a, hand_keys, 0)
 
     def hand_values(src_b):
         got(1, a * n2 + src_b)

time: 62 us -> 66.5 us (1.073)
  Pallas kernels: 58.9 us -> 63.4 us
    pallas_call x1, Pallas kernels: 58.9 us -> 63.4 us  [local(): pl.pallas_call(functools.partial(kernel, n, n1, n2), out_shape=(pltpu.VME...]
where the time goes in v3:
time: 66.5 us; the launch traced here: 66.4 us
  Pallas kernels  63.4 us (95%)
  local copies, waits for them, and re-layouts  2.29 us (3%)
    pallas_call x1, Pallas kernels, local(): pl.pallas_call(functools.partial(kernel, n, n1, n2), out_shape=(pltpu.VME...  63.4 us
    unnamed x2, local copies, waits for them, and re-layouts  2.29 us

profile of v3, /device:TPU:6, one launch (start us, length us, event | category | flops | bytes accessed | tf_op | source)
XLA Modules:
  0.0 66.4 jit_solution(4915562833174760992)
XLA Ops:
  0.6 63.4 %hybrid_cores.1 = (bf16[256,4096]{1,0:T(8,128)(2,1)S(1)}, bf16[256,2048]{1,0:T(8,128)(2,1)S(1)}) custom-call(bf16[256,4096]{1,0:T(8,128)(2,1)} %x_hbm.1, bf16[256,4096]{1,0:T(8,128)(2,1)} %gate_hbm.1, bf16[256,512]{1,0:T(8,128)(2,1)} %w_ref.1, bf16[256,512]{1,0:T(8,128)(2,1)} %r_hbm.1, f32[32,256]{1,0:T(8,128)} %bitcast.3, f32[1,32]{1,0:T(1,128)} %bitcast.5, ...), custom_call_target="tpu_custom_call" | custom-call | flops 4000000000 | bytes 12582912 | tf_op jit(solution)/shard_map/hybrid_cores/pallas_call | solution.py:571
  64.1 1.3 %copy.15 = bf16[256,4096]{1,0:T(8,128)(2,1)} copy(bf16[256,4096]{1,0:T(8,128)(2,1)S(1)} %get-tuple-element.2) | data formatting | bytes 4194304
  65.4 1.0 %copy.16 = bf16[256,2048]{1,0:T(8,128)(2,1)} copy(bf16[256,2048]{1,0:T(8,128)(2,1)S(1)} %get-tuple-element.3) | data formatting | bytes 2097152
